TPU v7x, 32 devices: a whole 2x2x4 slice. The times are simulated.
32 devices in a mesh: groups: 2 (over x), expert: 2 (over core), cuts: 8 (over z, y).
Axes of the slice: x: 2, y: 2, z: 4, core: 2. Of those that a mesh axis runs over, the one named last changes fastest.
Arguments:
- tokens: bfloat16 [1536, 6144], P(('groups', 'expert', 'cuts')), parts along dimension 0, may hold values from -6 to 6
- top_experts: int32 [1536, 2], P(('groups', 'expert', 'cuts')), parts along dimension 0, may hold values from 0 to 7, all different within a row; in each aligned block of 48 rows (0 to 47, 48 to 95, ...) at most 18 rows name the same one
- gate_fixed: int32 [1536, 2], P(('groups', 'expert', 'cuts')), parts along dimension 0, may hold values from 1 to 65535
- w_up: bfloat16 [2, 6144, 16384], P('expert', None, 'cuts'), may hold values from -0.078125 to 0.078125
- w_down: bfloat16 [2, 16384, 6144], P('expert', 'cuts'), may hold values from -0.046875 to 0.046875
Outputs:
- mixed: bfloat16 [1536, 6144], P(('groups', 'expert', 'cuts')), parts along dimension 0
There are 2 independent parts, one for each index of `groups`. A program takes and returns all parts, laid end to end along the dimension named above; an argument that names none is the same for every part. Nothing has to cross between parts.
Inputs may be any that keep to these rules, and one draw needn't show every extreme that they name: `top_experts`: each row names two different experts; the rows of one device name one expert at most 18 times.
All inputs are finite; a program needn't handle non-finite values.
Results may differ from a plain program's by a relative error of at most 0.0049.
Values may be sent and summed in bfloat16 or wider, within the bound.
A program may use at most 128 MiB of HBM per device.

v0:
```python
import jax
import jax.numpy as jnp
from jax import lax
from jax.sharding import PartitionSpec as P

CAP = 18


def slot_tables(top_experts, gate_fixed, experts):
    expert_ids = lax.broadcasted_iota(jnp.int32, (experts, 1, 1), 0)
    matched = top_experts[None, :, :] == expert_ids
    scaling = gate_fixed.astype(jnp.float32) * (1.0 / 65536.0)
    row_hit = jnp.any(matched, axis=2).astype(jnp.int32)
    row_gate = jnp.sum(jnp.where(matched, scaling[None, :, :], 0.0), axis=2)
    position = jnp.cumsum(row_hit, axis=1) - 1
    slot_ids = lax.broadcasted_iota(jnp.int32, (1, CAP, 1), 1)
    chosen = (position[:, None, :] == slot_ids) & (row_hit[:, None, :] > 0)
    weighted = jnp.where(chosen, row_gate[:, None, :], 0.0)
    return (chosen.astype(jnp.bfloat16), weighted)


def body(tokens, top_experts, gate_fixed, w_up, w_down):
    experts = lax.axis_size("expert")
    width = tokens.shape[1]
    select, weighted = slot_tables(top_experts, gate_fixed, experts)
    outgoing = jnp.einsum("jsr,rd->jsd", select, tokens, preferred_element_type=jnp.float32).astype(
        jnp.bfloat16
    )
    up_local = w_up[0]
    down_local = w_down[0]
    arrived = lax.all_to_all(outgoing, "expert", split_axis=0, concat_axis=0, tiled=True)
    hidden = jax.nn.gelu(
        jnp.dot(
            lax.all_gather(arrived.reshape(experts * CAP, width), "cuts", axis=0, tiled=True),
            up_local,
            preferred_element_type=jnp.float32,
        ),
        approximate=True,
    ).astype(jnp.bfloat16)
    summed = lax.psum_scatter(
        jnp.dot(hidden, down_local, preferred_element_type=jnp.float32),
        "cuts",
        scatter_dimension=0,
        tiled=True,
    ).reshape(experts, CAP, width)
    returned = lax.all_to_all(summed, "expert", split_axis=0, concat_axis=0, tiled=True)
    mixed = jnp.einsum("jsr,jsd->rd", weighted, returned, precision=lax.Precision.HIGHEST)
    return mixed.astype(jnp.bfloat16)


def solution(mesh):
    return jax.shard_map(
        body,
        mesh=mesh,
        in_specs=(
            P(("groups", "expert", "cuts"), None),
            P(("groups", "expert", "cuts"), None),
            P(("groups", "expert", "cuts"), None),
            P("expert", None, "cuts"),
            P("expert", "cuts", None),
        ),
        out_specs=P(("groups", "expert", "cuts"), None),
        check_vma=False,
    )
```

profile of v0, /device:TPU:13, one launch (start us, length us, event | category | flops | bytes accessed | tf_op | source)
XLA Modules:
  0.0 310.3 jit_solution(5143398973483312623)
XLA Ops:
  6.5 0.0 copy-start
  6.5 0.0 all-gather.3.cloned.1.call-start
  6.5 0.8 fusion.35
  7.3 0.2 reduce_window_sum.11
  7.5 0.1 copy-done
  7.6 0.3 convolution_convert_fusion
  7.9 4.5 %all_to_all.10 = bf16[2,18,6144]{2,1,0:T(8,128)(2,1)S(1)} all-to-all(bf16[2,18,6144]{2,1,0:T(8,128)(2,1)S(1)} %convolution_convert_fusion), channel_id=1, replica_groups=mesh['groups'=2,'expert'=2,'cuts'=8] {'expert'}, dimensions={0} | all-to-all | bytes 884736 | tf_op jit(solution)/shard_map/all_to_all | solution.py:31
  12.4 0.9 reshape.25
  13.3 0.0 all-gather.3.cloned.1.call-update
  13.3 68.3 %all-gather.3.cloned.1.call-done = bf16[8,36,6144]{2,1,0:T(8,128)(2,1)} async-done(((bf16[1,36,6144]{2,1,0:T(8,128)(2,1)}), bf16[8,36,6144]{2,1,0:T(8,128)(2,1)}) %all-gather.3.cloned.1.call-update) | async-done | bytes 3538960 | tf_op jit(solution)/shard_map/all_gather | solution.py:34
  81.7 4.7 %reshape.26 = bf16[288,6144]{1,0:T(8,128)(2,1)} reshape(bf16[8,36,6144]{2,1,0:T(8,128)(2,1)} %all-gather.3.cloned.1.call-done) | data formatting | bytes 7077888
  86.4 25.5 %fusion.1 = f32[288,6144]{1,0:T(8,128)} fusion(bf16[1,2048,6144]{2,1,0:T(8,128)(2,1)} %param.9, bf16[288,6144]{1,0:T(8,128)(2,1)} %reshape.26, bf16[1,6144,2048]{2,1,0:T(8,128)(2,1)} %param.8), kind=kOutput, calls=%fused_computation | convolution fusion | flops 14500823040 | bytes 60948480 | tf_op jit(solution)/shard_map/dot_general | solution.py:41
  111.9 0.0 copy-start.4
  111.9 0.0 copy-start.3
  111.9 0.0 copy-start.2
  111.9 158.2 %fusion = f32[40,6144]{1,0:T(8,128)S(1)} fusion(f32[288,6144]{1,0:T(8,128)} %fusion.1), kind=kCustom, calls=%all-reduce-scatter | all-reduce-scatter fusion | flops 1966081 | bytes 8061440
  270.1 0.1 slice
  270.2 1.9 collective-permute-start
  272.1 0.0 copy-done.4
  272.1 0.6 dynamic-slice.4
  273.4 0.0 copy-done.3
  273.4 0.0 copy-done.2
  273.4 15.9 %collective-permute-done = f32[28,6144]{1,0:T(8,128)} collective-permute-done((f32[28,6144]{1,0:T(8,128)S(1)}, f32[28,6144]{1,0:T(8,128)}, u32[]{:S(2)}, u32[]{:S(2)}) %collective-permute-start) | collective-permute-done | bytes 688160
  289.4 2.6 concatenate
  291.9 1.0 constant_dynamic-slice_fusion
  293.0 0.0 copy-start.1
  293.0 1.4 reshape.24
  294.4 7.1 %all_to_all.11 = f32[2,18,6144]{2,1,0:T(8,128)S(1)} all-to-all(f32[2,18,6144]{2,1,0:T(8,128)S(1)} %reshape.24), channel_id=1, replica_groups=mesh['groups'=2,'expert'=2,'cuts'=8] {'expert'}, dimensions={0} | all-to-all | bytes 1769472 | tf_op jit(solution)/shard_map/all_to_all | solution.py:46
  301.4 2.0 fusion.5
  303.4 0.0 copy-done.1
  (4 shorter events, 0.0 us)
Async XLA Ops:
  6.5 1.1 copy-start
  6.5 75.1 %all-gather.3.cloned.1.call-start = ((), (), s32[]{:S(2)}) async-start(), calls=%async_computation.2 | async-start | bytes 4423680 | tf_op jit(solution)/shard_map/all_gather | solution.py:34
  111.9 160.3 %copy-start.4 = (u32[32]{0:T(128)S(1)}, u32[32]{0:T(128)}, u32[]{:S(2)}) copy-start(u32[32]{0:T(128)} %constant.29) | copy-start | bytes 388
  111.9 161.5 %copy-start.3 = (s32[48,2]{0,1:T(2,128)S(1)}, s32[48,2]{0,1:T(2,128)}, u32[]{:S(2)}) copy-start(s32[48,2]{0,1:T(2,128)} %param.7) | copy-start | bytes 1156
  111.9 161.5 %copy-start.2 = (s32[48,2]{0,1:T(2,128)S(1)}, s32[48,2]{0,1:T(2,128)}, u32[]{:S(2)}) copy-start(s32[48,2]{0,1:T(2,128)} %param.6) | copy-start | bytes 1156
  270.2 19.2 %collective-permute-start = (f32[28,6144]{1,0:T(8,128)S(1)}, f32[28,6144]{1,0:T(8,128)}, u32[]{:S(2)}, u32[]{:S(2)}) collective-permute-start(f32[28,6144]{1,0:T(8,128)S(1)} %slice), channel_id=1, source_target_pairs={{0,1},{1,2},{2,3},{3,4},{4,5},{5,6},{6,7},{8,9},{9,10},{10,11},{11... | collective-permute-start | bytes 2064392
  293.0 10.4 %copy-start.1 = (bf16[48,6144]{1,0:T(8,128)(2,1)S(1)}, bf16[48,6144]{1,0:T(8,128)(2,1)}, u32[]{:S(2)}) copy-start(bf16[48,6144]{1,0:T(8,128)(2,1)} %param.5) | copy-start | bytes 1769476
Sparse Core Ops, SparseCore 0:
  13.5 68.1 all-gather.2
where the time goes:
time: 311 us; the launch traced here: 310 us
  blocking collectives  170 us (55%)
  waiting for transfers between devices  84.3 us (27%)
  matrix products  27.7 us (9%)
  between operations  14.1 us (5%)
  local copies, waits for them, and re-layouts  11.3 us (4%)
    unnamed x1, blocking collectives  158 us
    all_gather x1, waiting for transfers between devices, body(): lax.all_gather(arrived.reshape(experts * CAP, width), 'cuts', axis=0, til...  68.3 us
    dot_general x1, matrix products, body(): jnp.dot(hidden, down_local, preferred_element_type=jnp.float32)  25.5 us
    unnamed x2, waiting for transfers between devices  16 us
    unnamed x16, local copies, waits for them, and re-layouts  9.95 us
    all_to_all x1, blocking collectives, body(): lax.all_to_all(summed, 'expert', split_axis=0, concat_axis=0, tiled=True)  7.09 us
  transfers between devices with their start and end apart: 2, of which 2 were waited for; matrix products, arithmetic and copies ran while one was open for 0% of the time, Pallas kernels for 0%

commit v1 on v0

v1 whole, which is shorter than its diff:
```python
import functools

import jax
import jax.numpy as jnp
from jax import lax
from jax.experimental import pallas as pl
from jax.experimental.pallas import tpu as pltpu
from jax.sharding import PartitionSpec as P

F32, BF16 = jnp.float32, jnp.bfloat16
MAIN = 16
REST = 2
PARTS = 2
UPC = 256
DNC = 768
HELD = 6


def iota(shape, dim):
    return lax.broadcasted_iota(jnp.int32, shape, dim)


def kernel(
    Z, Y, half, fold,
    tok, top, gate, w_up, w_down, out,
    X, Xf, hid, wu, wd, stage, rcat, Yb, Rb, fin, fin_out,
    up_sem, dn_sem, sib_s, sib_r, ag_s, ag_r, y_s, y_r, rs_s, rs_r, fs, fr,
):
    e = lax.axis_index("expert")
    k = lax.axis_index("cuts")
    z, y = k // Y, k % Y
    devs = 2 * Z * Y
    rows = devs * MAIN
    extra = devs * REST
    nup, ndn = w_up.shape[1] // UPC, w_down.shape[1] // DNC
    per = ndn // PARTS
    folds = half // fold
    other = 1 - e

    def cup(i):
        return pltpu.make_async_copy(w_up.at[:, pl.ds(i * UPC, UPC)], wu.at[i], up_sem.at[i])

    def cdn(i):
        return pltpu.make_async_copy(
            w_down.at[:, pl.ds(i * DNC, DNC)], wd.at[i % HELD], dn_sem.at[i % HELD]
        )

    for i in range(nup):
        cup(i).start()
    for i in range(min(HELD, ndn)):
        cdn(i).start()

    barrier = pltpu.get_barrier_semaphore()
    cuts_up, cuts_down, cuts_y = (z + 1) * Y + y, (z - 1) * Y + y, z * Y + (Y - 1 - y)
    pl.semaphore_signal(barrier, inc=1, device_id={"expert": other})
    if Y == 2:
        pl.semaphore_signal(barrier, inc=1, device_id={"cuts": cuts_y})

    @pl.when(z < Z - 1)
    def _():
        pl.semaphore_signal(barrier, inc=1, device_id={"cuts": cuts_up})

    @pl.when(z > 0)
    def _():
        pl.semaphore_signal(barrier, inc=1, device_id={"cuts": cuts_down})

    n = tok.shape[0]
    tri = (iota((n, n), 0) <= iota((n, n), 1)).astype(F32).astype(BF16)
    hits, places, gates = [], [], []
    for x in range(2):
        m = (top[...] == x).astype(F32)
        hit = jnp.sum(m, axis=0, keepdims=True)
        g = jnp.sum(m * (gate[...].astype(F32) * (1.0 / 65536.0)), axis=0, keepdims=True)
        hb = jnp.broadcast_to(hit, (16, n)).astype(BF16)
        places.append(jnp.dot(hb, tri, preferred_element_type=F32)[0:1] - 1.0)
        hits.append(hit)
        gates.append(g)

    def pick(a, which):
        return jnp.where(which == 0, a[0], a[1])

    def select(which, slot):
        at = pick(places, which) == slot.astype(F32)
        return jnp.where(at & (pick(hits, which) > 0.5), 1.0, 0.0)

    ids = iota((MAIN, n), 0)
    mine = iota((MAIN, n), 0) * 0

    def fill(which, h, put):
        w = mine + which
        main = select(w, ids).astype(BF16)
        put(0, half, jnp.dot(main, tok[:, h * half:(h + 1) * half], preferred_element_type=F32).astype(BF16))
        acc = jnp.zeros((MAIN, fold), F32)
        rest = select(w, MAIN + ids // folds)
        for j in range(folds):
            sel = jnp.where(ids % folds == j, rest, 0.0).astype(BF16)
            lo = h * half + j * fold
            acc += jnp.dot(sel, tok[:, lo:lo + fold], preferred_element_type=F32)
        put(half, half + fold, acc.astype(BF16))

    def dev_of(zs, ys, c):
        return (zs * Y + ys) * 2 + c

    def sib(h):
        d = dev_of(z, y, e)
        return pltpu.make_async_remote_copy(
            stage.at[h], X.at[h, d], sib_s.at[h], sib_r.at[h], device_id={"expert": other}
        )

    def ag(d, h, dev):
        tgt = (cuts_up, cuts_down, cuts_y)[d]
        return pltpu.make_async_remote_copy(
            X.at[h, dev], X.at[h, dev], ag_s.at[d, h, dev], ag_r.at[h, dev], device_id={"cuts": tgt}
        )

    def ag_all(h, dev, act):
        @pl.when(z < Z - 1)
        def _():
            act(ag(0, h, dev))

        @pl.when(z > 0)
        def _():
            act(ag(1, h, dev))

        if Y == 2:
            act(ag(2, h, dev))

    def go(c):
        c.start()

    def sent(c):
        c.wait_send()

    own, sib_dev = dev_of(z, y, e), dev_of(z, y, other)
    for h in range(PARTS):
        def put(lo, hi, v):
            stage[h, :, lo:hi] = v

        fill(other, h, put)

    peers = 1 + (1 if Y == 2 else 0) + jnp.where(z < Z - 1, 1, 0) + jnp.where(z > 0, 1, 0)
    pl.semaphore_wait(barrier, peers)

    for h in range(PARTS):
        sib(h).start()
    for h in range(PARTS):
        def put(lo, hi, v):
            X[h, own, :, lo:hi] = v

        fill(e, h, put)
        ag_all(h, own, go)
    for h in range(PARTS):
        sib(h).wait_recv()
        ag_all(h, sib_dev, go)

    def relay(s, act, waits):
        @pl.when(z - s >= 0)
        def _():
            for h in range(PARTS):
                for c in range(2):
                    dev = dev_of(z - s, y, c)
                    if waits:
                        ag(0, h, dev).wait_recv()

                    @pl.when(z < Z - 1)
                    def _():
                        act(ag(0, h, dev))

                    if Y == 2:
                        act(ag(2, h, dev))

        @pl.when(z + s < Z)
        def _():
            for h in range(PARTS):
                for c in range(2):
                    dev = dev_of(z + s, y, c)
                    if waits:
                        ag(1, h, dev).wait_recv()

                    @pl.when(z > 0)
                    def _():
                        act(ag(1, h, dev))

                    if Y == 2:
                        act(ag(2, h, dev))

    @pl.loop(1, Z)
    def _(s):
        relay(s, go, True)

    if Y == 2:
        @pl.loop(0, Z)
        def _(zs):
            for h in range(PARTS):
                for c in range(2):
                    ag(2, h, dev_of(zs, 1 - y, c)).wait_recv()

    for h in range(PARTS):
        @pl.loop(0, devs)
        def _(d):
            Xf[pl.ds(pl.multiple_of(d * MAIN, MAIN), MAIN), h * half:(h + 1) * half] = X[h, d, :, 0:half]

    def unfold(shape, a, b):
        p, q = iota(shape, a), iota(shape, b)
        want = (q % folds) * extra + (q // MAIN) * REST + (q % MAIN) // folds
        return (p == want).astype(F32).astype(BF16)

    spread = unfold((rows, rows), 0, 1)
    for h in range(PARTS):
        got = jnp.dot(
            spread, X[h, :, :, half:].reshape(rows, fold), preferred_element_type=F32
        ).astype(BF16)
        for j in range(folds):
            lo = h * half + j * fold
            Xf[rows:, lo:lo + fold] = got[j * extra:(j + 1) * extra]

    @pl.loop(0, nup)
    def _(i):
        cup(i).wait()
        a = jnp.dot(Xf[...], wu[i], preferred_element_type=F32)
        hid[:, pl.ds(pl.multiple_of(i * UPC, UPC), UPC)] = jax.nn.gelu(a, approximate=True).astype(BF16)

    for h in range(PARTS):
        sib(h).wait_send()
        ag_all(h, own, sent)
        ag_all(h, sib_dev, sent)

    @pl.loop(1, Z)
    def _(s):
        relay(s, sent, False)

    def ycopy(h, zd, c):
        return pltpu.make_async_remote_copy(
            X.at[h, dev_of(zd, 1 - y, c)], Yb.at[h, zd, c], y_s.at[h, zd, c], y_r.at[h, zd, c],
            device_id={"cuts": cuts_y},
        )

    def rcopy(h, zd, slot, c, tgt):
        return pltpu.make_async_remote_copy(
            X.at[h, dev_of(zd, y, c)], Rb.at[h, slot, c], rs_s.at[h, slot, c], rs_r.at[h, slot, c],
            device_id={"cuts": tgt},
        )

    def far_first(act):
        @pl.loop(0, Z)
        def _(t):
            s = Z - 1 - t

            @pl.when(z + s < Z)
            def _():
                act(z + s)

            @pl.when((z - s >= 0) & (s > 0))
            def _():
                act(z - s)

    fold_in = unfold((rows, rows), 1, 0)
    for h in range(PARTS):
        @pl.loop(0, per)
        def _(t):
            i = h * per + t
            cdn(i).wait()
            a = jnp.dot(hid[...], wd[i % HELD], preferred_element_type=F32).astype(BF16)

            @pl.when(i + HELD < ndn)
            def _():
                cdn(i + HELD).start()

            X[h, :, :, pl.ds(pl.multiple_of(t * DNC, DNC), DNC)] = a[:rows].reshape(devs, MAIN, DNC)
            for j in range(DNC // fold):
                at = (t * (DNC // fold) + j) * extra
                rcat[pl.ds(pl.multiple_of(at, extra), extra), :] = a[rows:, j * fold:(j + 1) * fold]

        X[h, :, :, half:] = jnp.dot(
            fold_in, rcat[...], preferred_element_type=F32
        ).astype(BF16).reshape(devs, MAIN, fold)
        if Y == 2:
            def send_y(zd):
                for c in range(2):
                    ycopy(h, zd, c).start()

            far_first(send_y)

    def total(h, zd, c, slots):
        v = X[h, dev_of(zd, y, c)].astype(F32)
        if Y == 2:
            ycopy(h, zd, c).wait_recv()
            v += Yb[h, zd, c].astype(F32)
        return v

    def arrived(h, slot, c):
        rcopy(h, z, slot, c, cuts_up).wait_recv()
        return Rb[h, slot, c].astype(F32)

    def fcopy(h):
        return pltpu.make_async_remote_copy(
            fin_out.at[h], fin.at[h, e], fs.at[h], fr.at[h], device_id={"expert": other}
        )

    for h in range(PARTS):
        @pl.loop(0, Z - 1)
        def _(t):
            s = Z - 1 - t

            def hop(zd, slot, tgt, first):
                for c in range(2):
                    d = dev_of(zd, y, c)

                    v = total(h, zd, c, 0)

                    @pl.when(first)
                    def _():
                        X[h, d] = v.astype(BF16)

                    @pl.when(jnp.logical_not(first))
                    def _():
                        X[h, d] = (v + arrived(h, slot, c)).astype(BF16)

                    rcopy(h, zd, slot, c, tgt).start()

            @pl.when(z + s < Z)
            def _():
                hop(z + s, z + s + 1, cuts_up, z == 0)

            @pl.when(z - s >= 0)
            def _():
                hop(z - s, z - s, cuts_down, z == Z - 1)

        for which in range(2):
            c = (other, e)[which]
            dst = fin_out.at[h] if which == 0 else fin.at[h, e]
            dst[...] = total(h, z, c, 0)

            @pl.when(z > 0)
            def _():
                dst[...] += arrived(h, z + 1, c)

            @pl.when(z < Z - 1)
            def _():
                dst[...] += arrived(h, z, c)

            if which == 0:
                fcopy(h).start()

    q = iota((4 * MAIN, n), 0)
    which = (q // MAIN) % 2
    low = q < 2 * MAIN
    slot = jnp.where(low, q % MAIN, MAIN + (q % MAIN) // folds)
    weight = select(which, slot) * pick(gates, which)
    for h in range(PARTS):
        fcopy(h).wait()
        for j in range(folds):
            lhs = jnp.where(low | (q % folds == j), weight, 0.0)
            rhs = jnp.concatenate(
                [
                    fin[h, :, :, j * fold:(j + 1) * fold].reshape(2 * MAIN, fold),
                    fin[h, :, :, half:].reshape(2 * MAIN, fold),
                ],
                axis=0,
            )
            lo = h * half + j * fold
            out[:, lo:lo + fold] = lax.dot_general(
                lhs, rhs, (((0,), (0,)), ((), ())),
                precision=lax.Precision.HIGHEST, preferred_element_type=F32,
            ).astype(BF16)

    for h in range(PARTS):
        if Y == 2:
            @pl.loop(0, Z)
            def _(zd):
                for c in range(2):
                    ycopy(h, zd, c).wait_send()

        @pl.loop(1, Z)
        def _(s):
            @pl.when(z + s < Z)
            def _():
                for c in range(2):
                    rcopy(h, z + s, z + s + 1, c, cuts_up).wait_send()

            @pl.when(z - s >= 0)
            def _():
                for c in range(2):
                    rcopy(h, z - s, z - s, c, cuts_down).wait_send()


def body(Z, Y, tokens, top_experts, gate_fixed, w_up, w_down):
    n, width = tokens.shape
    units = w_up.shape[2]
    half = width // PARTS
    fold = half * REST // MAIN
    devs = 2 * Z * Y
    rows = devs * MAIN
    extra = devs * REST
    nup, ndn = units // UPC, width // DNC
    cols = half + fold
    DMA = pltpu.SemaphoreType.DMA
    vm = pl.BlockSpec(memory_space=pltpu.VMEM)
    anyw = pl.BlockSpec(memory_space=pl.ANY)
    return pl.pallas_call(
        functools.partial(kernel, Z, Y, half, fold),
        out_shape=jax.ShapeDtypeStruct((n, width), BF16),
        in_specs=[vm, vm, vm, anyw, anyw],
        out_specs=vm,
        scratch_shapes=[
            pltpu.VMEM((PARTS, devs, MAIN, cols), BF16),
            pltpu.VMEM((rows + extra, width), BF16),
            pltpu.VMEM((rows + extra, units), BF16),
            pltpu.VMEM((nup, width, UPC), BF16),
            pltpu.VMEM((HELD, units, DNC), BF16),
            pltpu.VMEM((PARTS, MAIN, cols), BF16),
            pltpu.VMEM((rows, fold), BF16),
            pltpu.VMEM((PARTS, Z, 2, MAIN, cols), BF16),
            pltpu.VMEM((PARTS, Z + 1, 2, MAIN, cols), BF16),
            pltpu.VMEM((PARTS, 2, MAIN, cols), F32),
            pltpu.VMEM((PARTS, MAIN, cols), F32),
            DMA((nup,)), DMA((HELD,)),
            DMA((PARTS,)), DMA((PARTS,)),
            DMA((3, PARTS, devs)), DMA((PARTS, devs)),
            DMA((PARTS, Z, 2)), DMA((PARTS, Z, 2)),
            DMA((PARTS, Z + 1, 2)), DMA((PARTS, Z + 1, 2)),
            DMA((PARTS,)), DMA((PARTS,)),
        ],
        compiler_params=pltpu.CompilerParams(
            collective_id=0, has_side_effects=True, vmem_limit_bytes=63 * 1024 * 1024
        ),
        cost_estimate=pl.CostEstimate(
            flops=4 * (rows + extra) * width * units,
            bytes_accessed=4 * width * units,
            transcendentals=(rows + extra) * units,
        ),
    )(tokens, top_experts.T, gate_fixed.T, w_up[0], w_down[0])


def solution(mesh):
    cuts = mesh.shape["cuts"]
    Y = 2 if cuts == 8 else 1
    return jax.shard_map(
        functools.partial(body, cuts // Y, Y),
        mesh=mesh,
        in_specs=(
            P(("groups", "expert", "cuts"), None),
            P(("groups", "expert", "cuts"), None),
            P(("groups", "expert", "cuts"), None),
            P("expert", None, "cuts"),
            P("expert", "cuts", None),
        ),
        out_specs=P(("groups", "expert", "cuts"), None),
        check_vma=False,
    )
```

time: 311 us -> 106 us (0.34)
  blocking collectives: 170 us -> 0 us
  Pallas kernels: 0 us -> 102 us
  waiting for transfers between devices: 84.3 us -> 0 us
  matrix products: 27.7 us -> 0 us
  between operations: 14.1 us -> 0.01 us
  local copies, waits for them, and re-layouts: 11.3 us -> 1.92 us
    unnamed x1 -> x0, blocking collectives: 158 us -> none
    pallas_call x0 -> x1, Pallas kernels: none -> 102 us  [body(): pl.pallas_call(functools.partial(kernel, Z, Y, half, fold), out_shape=jax...]
    all_gather x1 -> x0, waiting for transfers between devices: 68.3 us -> none  [body(): lax.all_gather(arrived.reshape(experts * CAP, width), 'cuts', axis=0, til...]
    dot_general x3 -> x0, matrix products: 27.7 us -> none  [the longest x1 25.5 us: body(): jnp.dot(hidden, down_local, preferred_element_type=jnp.float32)]
    unnamed x2 -> x0, waiting for transfers between devices: 16 us -> none
    all_to_all x2 -> x0, blocking collectives: 11.6 us -> none  [the longest x1 7.09 us: body(): lax.all_to_all(summed, 'expert', split_axis=0, concat_axis=0, tiled=True)]
    unnamed x16 -> x1, local copies, waits for them, and re-layouts: 9.95 us -> 1.92 us
  transfers between devices with their start and end apart: 2 -> 0, of which waited for: 2 -> 0; matrix products, arithmetic and copies ran while one was open for 0% -> 0% of each run, Pallas kernels for 0% -> 0%
where the time goes in v1:
time: 106 us; the launch traced here: 104 us
  Pallas kernels  102 us (96%)
  local copies, waits for them, and re-layouts  1.92 us (2%)
    pallas_call x1, Pallas kernels, body(): pl.pallas_call(functools.partial(kernel, Z, Y, half, fold), out_shape=jax...  102 us

profile of v1, /device:TPU:13, one launch (start us, length us, event | category | flops | bytes accessed | tf_op | source)
XLA Modules:
  0.0 103.9 jit_solution(3635125850281186158)
XLA Ops:
  0.0 102.0 %shard_map.55 = bf16[48,6144]{1,0:T(8,128)(2,1)} custom-call(bf16[48,6144]{1,0:T(8,128)(2,1)} %tok.1, s32[2,48]{1,0:T(2,128)} %bitcast.6, s32[2,48]{1,0:T(2,128)} %bitcast.7, bf16[6144,2048]{1,0:T(8,128)(2,1)} %bitcast.4, bf16[2048,6144]{1,0:T(8,128)(2,1)} %bitcast.5), custom_call_target="tpu_custom_call" | custom-call | flops 14495514624 | bytes 50331648 | tf_op jit(solution)/shard_map/pallas_call | solution.py:400
  102.0 1.9 %copy.7 = bf16[48,6144]{1,0:T(8,128)(2,1)} copy(bf16[48,6144]{1,0:T(8,128)(2,1)} %shard_map.55) | data formatting | bytes 1179648

commit v2 on v1

--- a/solution.py
+++ b/solution.py
@@ -10,10 +10,11 @@
 F32, BF16 = jnp.float32, jnp.bfloat16
 MAIN = 16
 REST = 2
-PARTS = 2
+PARTS = 3
+FIRST = 0
 UPC = 256
-DNC = 768
-HELD = 6
+DNC = 1024
+HELD = 4
 
 
 def iota(shape, dim):
@@ -23,7 +24,7 @@
 def kernel(
     Z, Y, half, fold,
     tok, top, gate, w_up, w_down, out,
-    X, Xf, hid, wu, wd, stage, rcat, Yb, Rb, fin, fin_out,
+    X, Xf, acc_up, hid, wu, wd, stage, rcat, Yb, Rb, fin, fin_out,
     up_sem, dn_sem, sib_s, sib_r, ag_s, ag_r, y_s, y_r, rs_s, rs_r, fs, fr,
 ):
     e = lax.axis_index("expert")
@@ -132,6 +133,8 @@
         c.wait_send()
 
     own, sib_dev = dev_of(z, y, e), dev_of(z, y, other)
+    early = FIRST if Y == 2 else 0
+
     for h in range(PARTS):
         def put(lo, hi, v):
             stage[h, :, lo:hi] = v
@@ -149,56 +152,76 @@
 
         fill(e, h, put)
         ag_all(h, own, go)
-    for h in range(PARTS):
+
+    @pl.loop(0, PARTS)
+    def _(h):
         sib(h).wait_recv()
         ag_all(h, sib_dev, go)
 
-    def relay(s, act, waits):
-        @pl.when(z - s >= 0)
+    def along(h, dev, act):
+        @pl.when(z < Z - 1)
         def _():
-            for h in range(PARTS):
-                for c in range(2):
-                    dev = dev_of(z - s, y, c)
-                    if waits:
-                        ag(0, h, dev).wait_recv()
-
-                    @pl.when(z < Z - 1)
+            act(ag(0, h, dev))
+
+        @pl.when(z > 0)
+        def _():
+            act(ag(1, h, dev))
+
+    def crossed(act, waits):
+        for h in range(early):
+            for c in range(2):
+                dev = dev_of(z, 1 - y, c)
+                if waits:
+                    ag(2, h, dev).wait_recv()
+                along(h, dev, act)
+
+    def relay(h, s, ys, cross, act, waits):
+        for c in range(2):
+            @pl.when(z - s >= 0)
+            def _():
+                dev = dev_of(z - s, ys, c)
+                if waits:
+                    ag(0, h, dev).wait_recv()
+
+                @pl.when(z < Z - 1)
+                def _():
+                    act(ag(0, h, dev))
+
+                if cross:
+                    act(ag(2, h, dev))
+
+            @pl.when(z + s < Z)
+            def _():
+                dev = dev_of(z + s, ys, c)
+                if waits:
+                    ag(1, h, dev).wait_recv()
+
+                @pl.when(z > 0)
+                def _():
+                    act(ag(1, h, dev))
+
+                if cross:
+                    act(ag(2, h, dev))
+
+    def relays(act, waits):
+        @pl.loop(0, PARTS + Z - 2)
+        def _(t):
+            @pl.loop(1, Z)
+            def _(s):
+                h = t - (s - 1)
+
+                @pl.when((h >= early) & (h < PARTS))
+                def _():
+                    relay(h, s, y, Y == 2, act, waits)
+
+                if early:
+                    @pl.when((h >= 0) & (h < early))
                     def _():
-                        act(ag(0, h, dev))
-
-                    if Y == 2:
-                        act(ag(2, h, dev))
-
-        @pl.when(z + s < Z)
-        def _():
-            for h in range(PARTS):
-                for c in range(2):
-                    dev = dev_of(z + s, y, c)
-                    if waits:
-                        ag(1, h, dev).wait_recv()
-
-                    @pl.when(z > 0)
-                    def _():
-                        act(ag(1, h, dev))
-
-                    if Y == 2:
-                        act(ag(2, h, dev))
-
-    @pl.loop(1, Z)
-    def _(s):
-        relay(s, go, True)
-
-    if Y == 2:
-        @pl.loop(0, Z)
-        def _(zs):
-            for h in range(PARTS):
-                for c in range(2):
-                    ag(2, h, dev_of(zs, 1 - y, c)).wait_recv()
-
-    for h in range(PARTS):
-        @pl.loop(0, devs)
-        def _(d):
-            Xf[pl.ds(pl.multiple_of(d * MAIN, MAIN), MAIN), h * half:(h + 1) * half] = X[h, d, :, 0:half]
+                        relay(h, s, y, False, act, waits)
+                        relay(h, s, 1 - y, False, act, waits)
+
+    crossed(go, True)
+    relays(go, True)
 
     def unfold(shape, a, b):
         p, q = iota(shape, a), iota(shape, b)
@@ -207,27 +230,43 @@
 
     spread = unfold((rows, rows), 0, 1)
     for h in range(PARTS):
+        if Y == 2 and h >= early:
+            @pl.loop(0, Z)
+            def _(zs):
+                for c in range(2):
+                    ag(2, h, dev_of(zs, 1 - y, c)).wait_recv()
+
+        @pl.loop(0, devs)
+        def _(d):
+            Xf[pl.ds(pl.multiple_of(d * MAIN, MAIN), MAIN), :] = X[h, d, :, 0:half]
+
         got = jnp.dot(
             spread, X[h, :, :, half:].reshape(rows, fold), preferred_element_type=F32
         ).astype(BF16)
         for j in range(folds):
-            lo = h * half + j * fold
-            Xf[rows:, lo:lo + fold] = got[j * extra:(j + 1) * extra]
-
-    @pl.loop(0, nup)
-    def _(i):
-        cup(i).wait()
-        a = jnp.dot(Xf[...], wu[i], preferred_element_type=F32)
-        hid[:, pl.ds(pl.multiple_of(i * UPC, UPC), UPC)] = jax.nn.gelu(a, approximate=True).astype(BF16)
-
-    for h in range(PARTS):
+            Xf[rows:, j * fold:(j + 1) * fold] = got[j * extra:(j + 1) * extra]
+
+        @pl.loop(0, nup)
+        def _(i):
+            if h == 0:
+                cup(i).wait()
+            a = jnp.dot(Xf[...], wu[i, h * half:(h + 1) * half, :], preferred_element_type=F32)
+            at = pl.ds(pl.multiple_of(i * UPC, UPC), UPC)
+            if h > 0:
+                a += acc_up[:, at]
+            if h < PARTS - 1:
+                acc_up[:, at] = a
+            else:
+                hid[:, at] = jax.nn.gelu(a, approximate=True).astype(BF16)
+
+    @pl.loop(0, PARTS)
+    def _(h):
         sib(h).wait_send()
         ag_all(h, own, sent)
         ag_all(h, sib_dev, sent)
 
-    @pl.loop(1, Z)
-    def _(s):
-        relay(s, sent, False)
+    crossed(sent, False)
+    relays(sent, False)
 
     def ycopy(h, zd, c):
         return pltpu.make_async_remote_copy(
@@ -235,24 +274,23 @@
             device_id={"cuts": cuts_y},
         )
 
-    def rcopy(h, zd, slot, c, tgt):
+    def rcopy(h, zd, over, slot, c, tgt):
+        ys = 1 - y if over else y
+        at = over * 2 + c
         return pltpu.make_async_remote_copy(
-            X.at[h, dev_of(zd, y, c)], Rb.at[h, slot, c], rs_s.at[h, slot, c], rs_r.at[h, slot, c],
+            X.at[h, dev_of(zd, ys, c)], Rb.at[h, slot, at], rs_s.at[h, slot, at], rs_r.at[h, slot, at],
             device_id={"cuts": tgt},
         )
 
-    def far_first(act):
-        @pl.loop(0, Z)
-        def _(t):
-            s = Z - 1 - t
-
+    def send_y(h, s):
+        for c in range(2):
             @pl.when(z + s < Z)
             def _():
-                act(z + s)
+                ycopy(h, z + s, c).start()
 
             @pl.when((z - s >= 0) & (s > 0))
             def _():
-                act(z - s)
+                ycopy(h, z - s, c).start()
 
     fold_in = unfold((rows, rows), 1, 0)
     for h in range(PARTS):
@@ -274,73 +312,110 @@
         X[h, :, :, half:] = jnp.dot(
             fold_in, rcat[...], preferred_element_type=F32
         ).astype(BF16).reshape(devs, MAIN, fold)
-        if Y == 2:
-            def send_y(zd):
-                for c in range(2):
-                    ycopy(h, zd, c).start()
-
-            far_first(send_y)
-
-    def total(h, zd, c, slots):
+        if Y == 2 and h >= early:
+            @pl.loop(0, Z - 2)
+            def _(t):
+                send_y(h, Z - 1 - t)
+
+    if Y == 2:
+        for s in (1, 0):
+            @pl.loop(early, PARTS)
+            def _(h):
+                send_y(h, s)
+
+    def total(h, zd, c, crosses):
         v = X[h, dev_of(zd, y, c)].astype(F32)
-        if Y == 2:
+        if crosses:
             ycopy(h, zd, c).wait_recv()
             v += Yb[h, zd, c].astype(F32)
         return v
 
-    def arrived(h, slot, c):
-        rcopy(h, z, slot, c, cuts_up).wait_recv()
-        return Rb[h, slot, c].astype(F32)
+    def arrived(h, over, slot, c):
+        rcopy(h, z, over, slot, c, cuts_up).wait_recv()
+        return Rb[h, slot, over * 2 + c].astype(F32)
 
     def fcopy(h):
         return pltpu.make_async_remote_copy(
             fin_out.at[h], fin.at[h, e], fs.at[h], fr.at[h], device_id={"expert": other}
         )
 
-    for h in range(PARTS):
-        @pl.loop(0, Z - 1)
-        def _(t):
-            s = Z - 1 - t
-
-            def hop(zd, slot, tgt, first):
-                for c in range(2):
-                    d = dev_of(zd, y, c)
-
-                    v = total(h, zd, c, 0)
-
-                    @pl.when(first)
-                    def _():
-                        X[h, d] = v.astype(BF16)
-
-                    @pl.when(jnp.logical_not(first))
-                    def _():
-                        X[h, d] = (v + arrived(h, slot, c)).astype(BF16)
-
-                    rcopy(h, zd, slot, c, tgt).start()
-
-            @pl.when(z + s < Z)
-            def _():
-                hop(z + s, z + s + 1, cuts_up, z == 0)
-
-            @pl.when(z - s >= 0)
-            def _():
-                hop(z - s, z - s, cuts_down, z == Z - 1)
-
+    def hop(h, zd, over, crosses, slot, tgt, opens):
+        for c in range(2):
+            d = dev_of(zd, 1 - y if over else y, c)
+            if crosses:
+                v = total(h, zd, c, True)
+
+                @pl.when(opens)
+                def _():
+                    X[h, d] = v.astype(BF16)
+
+                @pl.when(jnp.logical_not(opens))
+                def _():
+                    X[h, d] = (v + arrived(h, over, slot, c)).astype(BF16)
+            else:
+                @pl.when(jnp.logical_not(opens))
+                def _():
+                    X[h, d] = (X[h, d].astype(F32) + arrived(h, over, slot, c)).astype(BF16)
+
+            rcopy(h, zd, over, slot, c, tgt).start()
+
+    def hops(h, s, over, crosses):
+        @pl.when(z + s < Z)
+        def _():
+            hop(h, z + s, over, crosses, z + s + 1, cuts_up, z == 0)
+
+        @pl.when(z - s >= 0)
+        def _():
+            hop(h, z - s, over, crosses, z - s, cuts_down, z == Z - 1)
+
+    @pl.loop(0, Z - 1)
+    def _(t):
+        s = Z - 1 - t
+        for h in range(early):
+            hops(h, s, 1, False)
+            hops(h, s, 0, False)
+
+        @pl.loop(early, PARTS)
+        def _(h):
+            hops(h, s, 0, Y == 2)
+
+    for h in range(early):
+        for c in range(2):
+            d = dev_of(z, 1 - y, c)
+
+            @pl.when(z > 0)
+            def _():
+                X[h, d] = (X[h, d].astype(F32) + arrived(h, 1, z + 1, c)).astype(BF16)
+
+            @pl.when(z < Z - 1)
+            def _():
+                X[h, d] = (X[h, d].astype(F32) + arrived(h, 1, z, c)).astype(BF16)
+
+            ycopy(h, z, c).start()
+
+    def finish(h):
         for which in range(2):
             c = (other, e)[which]
             dst = fin_out.at[h] if which == 0 else fin.at[h, e]
-            dst[...] = total(h, z, c, 0)
+            dst[...] = total(h, z, c, Y == 2)
 
             @pl.when(z > 0)
             def _():
-                dst[...] += arrived(h, z + 1, c)
+                dst[...] += arrived(h, 0, z + 1, c)
 
             @pl.when(z < Z - 1)
             def _():
-                dst[...] += arrived(h, z, c)
+                dst[...] += arrived(h, 0, z, c)
 
             if which == 0:
                 fcopy(h).start()
+
+    @pl.loop(early, PARTS)
+    def _(h):
+        finish(h)
+
+    for h in range(early):
+        finish(h)
 
     q = iota((4 * MAIN, n), 0)
     which = (q // MAIN) % 2
@@ -364,24 +439,34 @@
                 precision=lax.Precision.HIGHEST, preferred_element_type=F32,
             ).astype(BF16)
 
-    for h in range(PARTS):
-        if Y == 2:
+    def rs_sent(h, over):
+        @pl.loop(1, Z)
+        def _(s):
+            for c in range(2):
+                @pl.when(z + s < Z)
+                def _():
+                    rcopy(h, z + s, over, z + s + 1, c, cuts_up).wait_send()
+
+                @pl.when(z - s >= 0)
+                def _():
+                    rcopy(h, z - s, over, z - s, c, cuts_down).wait_send()
+
+    @pl.loop(0, PARTS)
+    def _(h):
+        rs_sent(h, 0)
+
+    for h in range(early):
+        rs_sent(h, 1)
+        for c in range(2):
+            ycopy(h, z, c).wait_send()
+
+    if Y == 2:
+        @pl.loop(early, PARTS)
+        def _(h):
             @pl.loop(0, Z)
             def _(zd):
                 for c in range(2):
                     ycopy(h, zd, c).wait_send()
-
-        @pl.loop(1, Z)
-        def _(s):
-            @pl.when(z + s < Z)
-            def _():
-                for c in range(2):
-                    rcopy(h, z + s, z + s + 1, c, cuts_up).wait_send()
-
-            @pl.when(z - s >= 0)
-            def _():
-                for c in range(2):
-                    rcopy(h, z - s, z - s, c, cuts_down).wait_send()
 
 
 def body(Z, Y, tokens, top_experts, gate_fixed, w_up, w_down):
@@ -404,21 +489,22 @@
         out_specs=vm,
         scratch_shapes=[
             pltpu.VMEM((PARTS, devs, MAIN, cols), BF16),
-            pltpu.VMEM((rows + extra, width), BF16),
+            pltpu.VMEM((rows + extra, half), BF16),
+            pltpu.VMEM((rows + extra, units), F32),
             pltpu.VMEM((rows + extra, units), BF16),
             pltpu.VMEM((nup, width, UPC), BF16),
             pltpu.VMEM((HELD, units, DNC), BF16),
             pltpu.VMEM((PARTS, MAIN, cols), BF16),
             pltpu.VMEM((rows, fold), BF16),
             pltpu.VMEM((PARTS, Z, 2, MAIN, cols), BF16),
-            pltpu.VMEM((PARTS, Z + 1, 2, MAIN, cols), BF16),
+            pltpu.VMEM((PARTS, Z + 1, 2 * Y, MAIN, cols), BF16),
             pltpu.VMEM((PARTS, 2, MAIN, cols), F32),
             pltpu.VMEM((PARTS, MAIN, cols), F32),
             DMA((nup,)), DMA((HELD,)),
             DMA((PARTS,)), DMA((PARTS,)),
             DMA((3, PARTS, devs)), DMA((PARTS, devs)),
             DMA((PARTS, Z, 2)), DMA((PARTS, Z, 2)),
-            DMA((PARTS, Z + 1, 2)), DMA((PARTS, Z + 1, 2)),
+            DMA((PARTS, Z + 1, 2 * Y)), DMA((PARTS, Z + 1, 2 * Y)),
             DMA((PARTS,)), DMA((PARTS,)),
         ],
         compiler_params=pltpu.CompilerParams(

time: 106 us -> 100 us (0.943); the launches traced: 104 us -> 99.8 us
  Pallas kernels: 102 us -> 97.8 us
    pallas_call x1, Pallas kernels: 102 us -> 97.8 us  [body(): pl.pallas_call(functools.partial(kernel, Z, Y, half, fold), out_shape=jax...]
where the time goes in v2:
time: 100 us; the launch traced here: 99.8 us
  Pallas kernels  97.8 us (98%)
  local copies, waits for them, and re-layouts  1.92 us (2%)
    pallas_call x1, Pallas kernels, body(): pl.pallas_call(functools.partial(kernel, Z, Y, half, fold), out_shape=jax...  97.8 us

profile of v2, /device:TPU:13, one launch (start us, length us, event | category | flops | bytes accessed | tf_op | source)
XLA Modules:
  0.0 99.8 jit_solution(10321732227651177060)
XLA Ops:
  0.0 97.8 %shard_map.55 = bf16[48,6144]{1,0:T(8,128)(2,1)} custom-call(bf16[48,6144]{1,0:T(8,128)(2,1)} %tok.1, s32[2,48]{1,0:T(2,128)} %bitcast.6, s32[2,48]{1,0:T(2,128)} %bitcast.7, bf16[6144,2048]{1,0:T(8,128)(2,1)} %bitcast.4, bf16[2048,6144]{1,0:T(8,128)(2,1)} %bitcast.5), custom_call_target="tpu_custom_call" | custom-call | flops 14495514624 | bytes 50331648 | tf_op jit(solution)/shard_map/pallas_call | solution.py:485
  97.9 1.9 %copy.7 = bf16[48,6144]{1,0:T(8,128)(2,1)} copy(bf16[48,6144]{1,0:T(8,128)(2,1)} %shard_map.55) | data formatting | bytes 1179648

commit v3 on v2

--- a/solution.py
+++ b/solution.py
@@ -46,11 +46,6 @@
             w_down.at[:, pl.ds(i * DNC, DNC)], wd.at[i % HELD], dn_sem.at[i % HELD]
         )
 
-    for i in range(nup):
-        cup(i).start()
-    for i in range(min(HELD, ndn)):
-        cdn(i).start()
-
     barrier = pltpu.get_barrier_semaphore()
     cuts_up, cuts_down, cuts_y = (z + 1) * Y + y, (z - 1) * Y + y, z * Y + (Y - 1 - y)
     pl.semaphore_signal(barrier, inc=1, device_id={"expert": other})
@@ -219,6 +214,11 @@
                     def _():
                         relay(h, s, y, False, act, waits)
                         relay(h, s, 1 - y, False, act, waits)
+
+    for i in range(nup):
+        cup(i).start()
+    for i in range(min(HELD, ndn)):
+        cdn(i).start()
 
     crossed(go, True)
     relays(go, True)

time: 100 us -> 100 us (level)
  no operation moved by 1% of the time
where the time goes in v3:
time: 100 us; the launch traced here: 99.8 us
  Pallas kernels  97.9 us (98%)
  local copies, waits for them, and re-layouts  1.92 us (2%)
    pallas_call x1, Pallas kernels, body(): pl.pallas_call(functools.partial(kernel, Z, Y, half, fold), out_shape=jax...  97.9 us

profile of v3, /device:TPU:13, one launch (start us, length us, event | category | flops | bytes accessed | tf_op | source)
XLA Modules:
  0.0 99.8 jit_solution(10414230469204645735)
XLA Ops:
  0.0 97.9 %shard_map.55 = bf16[48,6144]{1,0:T(8,128)(2,1)} custom-call(bf16[48,6144]{1,0:T(8,128)(2,1)} %tok.1, s32[2,48]{1,0:T(2,128)} %bitcast.6, s32[2,48]{1,0:T(2,128)} %bitcast.7, bf16[6144,2048]{1,0:T(8,128)(2,1)} %bitcast.4, bf16[2048,6144]{1,0:T(8,128)(2,1)} %bitcast.5), custom_call_target="tpu_custom_call" | custom-call | flops 14495514624 | bytes 50331648 | tf_op jit(solution)/shard_map/pallas_call | solution.py:485
  97.9 1.9 %copy.7 = bf16[48,6144]{1,0:T(8,128)(2,1)} copy(bf16[48,6144]{1,0:T(8,128)(2,1)} %shard_map.55) | data formatting | bytes 1179648
